TPU v7x, 32 devices: a whole 2x2x4 slice. The times are simulated.
32 devices in a mesh: gx: 8 (over z, core), gy: 4 (over y, x).
Axes of the slice: x: 2, y: 2, z: 4, core: 2. Of those that a mesh axis runs over, the one named last changes fastest.
Arguments:
- demand: float32 [16, 1024, 16384], P(None, 'gx', 'gy'), may hold values from -200 to 200, as said below
- initial: float32 [1024, 256], replicated, may hold values from -6 to 6
Outputs:
- factor: float32 [1024, 256], replicated
- core: float32 [256, 16, 16384], P('gx', None, 'gy')
Inputs may be any that keep to these rules, and one draw needn't show every extreme that they name: `demand`: Real-valued fluctuations of order one to a few, not all of one scale along x.
All inputs are finite; a program needn't handle non-finite values.
Results may differ from a plain program's by a relative error of at most 0.0003.
Values sent between devices are 32-bit elements; how exact they have to be, the bound alone decides.
A program may use at most 128 MiB of HBM per device.

v0:
```python
import jax
import jax.numpy as jnp
from jax import lax
from jax.sharding import PartitionSpec as P

NY = 1024
L = 16
S = 16
ITERS = 3


def orthonormal(block):
    weights = jnp.dot(
        block.T, block, precision=lax.Precision.HIGHEST, preferred_element_type=jnp.float32
    )
    lower_factor = jnp.linalg.cholesky(weights)
    return lax.linalg.triangular_solve(
        lower_factor, block, left_side=False, lower=True, transpose_a=True
    )


def on_device(demand, initial):
    regrouped = lax.all_to_all(demand, "gx", split_axis=0, concat_axis=1, tiled=True)
    local_gram = jnp.einsum(
        "lxc,lzc->xz",
        regrouped,
        regrouped,
        precision=lax.Precision.HIGHEST,
        preferred_element_type=jnp.float32,
    )
    local_gram = local_gram * (1.0 / (L * S * NY))
    basis = initial
    gram = lax.psum(local_gram, ("gx", "gy"))
    for iteration in range(ITERS):
        basis = orthonormal(
            jnp.dot(
                gram, basis, precision=lax.Precision.HIGHEST, preferred_element_type=jnp.float32
            )
        )
    core_part = jnp.einsum(
        "xr,lxc->rlc",
        basis,
        regrouped,
        precision=lax.Precision.HIGHEST,
        preferred_element_type=jnp.float32,
    )
    core = lax.all_to_all(core_part, "gx", split_axis=0, concat_axis=1, tiled=True)
    return (basis, core)


def solution(mesh):
    in_specs = (P(None, "gx", "gy"), P())
    out_specs = (P(), P("gx", None, "gy"))
    return jax.shard_map(
        on_device, mesh=mesh, in_specs=in_specs, out_specs=out_specs, check_vma=False
    )
```

profile of v0, /device:TPU:16, one launch (start us, length us, event | category | flops | bytes accessed | tf_op | source)
XLA Modules:
  0.0 1479.7 jit_solution(2517403497320483038)
XLA Ops:
  7.2 726.9 %all_to_all.36 = f32[16,128,4096]{2,1,0:T(8,128)S(1)} all-to-all(f32[16,128,4096]{2,1,0:T(8,128)} %param.5), channel_id=1, replica_groups=mesh['gx'=8,'gy'=4] {'gx'}, dimensions={0} | all-to-all | bytes 67108864 | tf_op jit(solution)/shard_map/all_to_all | solution.py:23
  734.1 11.0 copy.10
  745.1 115.4 %bitcast_multiply_fusion = f32[1024,1024]{1,0:T(8,128)} fusion(f32[2,1024,4096]{2,1,0:T(8,128)} %bitcast.121), kind=kOutput, calls=%fused_computation.6 | convolution fusion | flops 103080263680 | bytes 37748736 | tf_op jit(solution)/shard_map/lxc,lzc->xz/dot_general | solution.py:24
  860.6 141.9 %all-reduce.3.cloned.1.call-done = f32[1024,1024]{1,0:T(8,128)} async-done(((f32[1024,1024]{1,0:T(8,128)}), f32[1024,1024]{1,0:T(8,128)}) %all-reduce.3.cloned.1.call-update) | async-done | bytes 4194320 | tf_op jit(solution)/shard_map/psum | solution.py:33
  1002.5 5.5 fusion.47
  1010.1 11.7 cholesky.172
  1021.8 9.8 custom-call.15
  1032.1 11.7 cholesky.189
  1062.8 19.7 %custom-call.16 = f32[2,128,128]{1,2,0:T(8,128)S(1)} custom-call(f32[2,128,128]{2,1,0:T(8,128)S(1)} %get-tuple-element.24), custom_call_target="InvertDiagBlocksLowerTriangular" | custom-call | tf_op jit(solution)/shard_map/triangular_solve/custom-call.0 | solution.py:17
  1092.1 11.7 cholesky.206
  1103.9 9.8 custom-call.17
  1114.2 11.7 cholesky.223
  1132.7 19.7 %custom-call.18 = f32[2,128,128]{1,2,0:T(8,128)S(1)} custom-call(f32[2,128,128]{2,1,0:T(8,128)S(1)} %get-tuple-element.25), custom_call_target="InvertDiagBlocksLowerTriangular" | custom-call | tf_op jit(solution)/shard_map/triangular_solve/custom-call.0 | solution.py:17
  1154.7 5.5 fusion.4
  1162.2 11.7 cholesky.240
  1174.0 9.8 custom-call.19
  1184.3 11.7 cholesky.257
  1203.0 19.7 %custom-call.20 = f32[2,128,128]{1,2,0:T(8,128)S(1)} custom-call(f32[2,128,128]{2,1,0:T(8,128)S(1)} %get-tuple-element.26), custom_call_target="InvertDiagBlocksLowerTriangular" | custom-call | tf_op jit(solution)/shard_map/triangular_solve/custom-call.0 | solution.py:17
  1225.0 32.3 %fusion.8 = f32[256,2,4096]{2,0,1:T(8,128)S(1)} fusion(f32[2,1024,4096]{2,1,0:T(8,128)} %bitcast.122, f32[1024,128]{0,1:T(8,128)S(1)} %fusion.19, f32[1024,128]{0,1:T(8,128)S(1)} %bitcast.124), kind=kOutput, calls=%fused_computation.22 | convolution fusion | flops 25770065920 | bytes 42991616 | tf_op jit(solution)/shard_map/xr,lxc->rlc/dot_general | solution.py:40
  1257.3 10.1 copy.14
  1267.4 6.3 all-to-all-start.1
  1277.4 176.9 %all-to-all-done.1 = f32[256,2,4096]{2,1,0:T(2,128)} async-done(((f32[256,2,4096]{2,1,0:T(2,128)}), f32[256,2,4096]{2,1,0:T(2,128)}, u32[]{:S(2)}, u32[]{:S(2)}) %all-to-all-start.1) | async-done | bytes 8388640 | tf_op jit(solution)/shard_map/all_to_all | solution.py:47
  1454.3 7.4 copy.15
  1461.7 10.9 all_to_all.33
  (77 shorter events, 51.2 us)
Async XLA Ops:
  7.2 995.4 %copy-start = (f32[1024,256]{1,0:T(8,128)S(1)}, f32[1024,256]{1,0:T(8,128)}, u32[]{:S(2)}) copy-start(f32[1024,256]{1,0:T(8,128)} %param.6) | copy-start | bytes 3145732
  7.2 995.4 %all-reduce.3.cloned.1.call-start = ((), (), s32[]{:S(2)}) async-start(), calls=%async_computation.2 | async-start | bytes 8388608 | tf_op jit(solution)/shard_map/psum | solution.py:33
  1267.4 187.0 %all-to-all-start.1 = ((f32[256,2,4096]{2,1,0:T(2,128)}), f32[256,2,4096]{2,1,0:T(2,128)}, u32[]{:S(2)}, u32[]{:S(2)}) async-start(f32[256,2,4096]{2,1,0:T(2,128)} %copy.14), calls=%async_computation.1 | async-start | bytes 16777216 | tf_op jit(solution)/shard_map/all_to_all | solution.py:47
Sparse Core Ops, SparseCore 0:
  860.7 141.7 all-reduce.2
where the time goes:
time: 1490 us; the launch traced here: 1480 us
  blocking collectives  727 us (49%)
  waiting for transfers between devices  319 us (21%)
  matrix products  178 us (12%)
  other arithmetic  164 us (11%)
  local copies, waits for them, and re-layouts  54.2 us (4%)
  between operations  31.3 us (2%)
    all_to_all x1, blocking collectives, on_device(): lax.all_to_all(demand, 'gx', split_axis=0, concat_axis=1, tiled=True)  727 us
    all_to_all x1, waiting for transfers between devices, on_device(): lax.all_to_all(core_part, 'gx', split_axis=0, concat_axis=1, tiled=True)  177 us
    psum x1, waiting for transfers between devices, on_device(): gram = lax.psum(local_gram, ('gx', 'gy'))  142 us
    dot_general x1, matrix products, on_device(): jnp.einsum('lxc,lzc->xz', regrouped, regrouped, precision=lax.Precision.H...  115 us
    another operation x20, other arithmetic, orthonormal(): lower_factor = jnp.linalg.cholesky(weights)  103 us
    another operation x8, other arithmetic, orthonormal(): lax.linalg.triangular_solve(lower_factor, block, left_side=False, lower=T...  60.9 us
    dot_general x1, matrix products, on_device(): jnp.einsum('xr,lxc->rlc', basis, regrouped, precision=lax.Precision.HIGHE...  32.3 us
  transfers between devices with their start and end apart: 2, of which 2 were waited for; matrix products, arithmetic and copies ran while one was open for 0% of the time, Pallas kernels for 0%

commit v1 on v0

v1 whole, which is shorter than its diff:
```python
import functools

import jax
import jax.numpy as jnp
from jax import lax
from jax.experimental import pallas as pl
from jax.experimental.pallas import tpu as pltpu
from jax.sharding import PartitionSpec as P

ITERS = 3
TILE = 256
PANEL = 32
WINDOW = 3
MESH = pl.DeviceIdType.MESH
HIGHEST = lax.Precision.HIGHEST


def dot(left, right, dims):
    return lax.dot_general(
        left, right, (dims, ((), ())), precision=HIGHEST, preferred_element_type=jnp.float32
    )


def chunk_columns(layers, columns):
    return min(columns, max(128, layers * columns // 8))


def far_first(n):
    return sorted(range(1, n), key=lambda p: (abs(p - n // 2), p))


def enter(n, me):
    barrier = pltpu.get_barrier_semaphore()
    for p in range(1, n):
        pl.semaphore_signal(
            barrier, inc=1, device_id={"gx": lax.rem(me + p, n)}, device_id_type=MESH
        )
    pl.semaphore_wait(barrier, n - 1)


def exchange_gram_kernel(
    n, layers, width, scale, demand, regrouped, gram, block, send_sems, recv_sems, self_sem, load_sem
):
    me = lax.axis_index("gx")
    rows, columns = demand.shape[1], demand.shape[2]
    per_layer = columns // width
    chunks = layers * per_layer
    order = far_first(n)

    def place(c):
        return lax.div(c, per_layer), pl.multiple_of(lax.rem(c, per_layer) * width, width)

    def outgoing(c, p):
        layer, column = place(c)
        target = lax.rem(me + p, n)
        return pltpu.make_async_remote_copy(
            src_ref=demand.at[target * layers + layer, :, pl.ds(column, width)],
            dst_ref=regrouped.at[layer, pl.ds(pl.multiple_of(me * rows, rows), rows), pl.ds(column, width)],
            send_sem=send_sems.at[c, p - 1],
            recv_sem=recv_sems.at[c, p - 1],
            device_id={"gx": target},
            device_id_type=MESH,
        )

    def send(c):
        for p in order:
            outgoing(c, p).start()

    enter(n, me)
    for c in range(min(WINDOW, chunks)):
        send(jnp.int32(c))
    own = pltpu.make_async_copy(
        demand.at[pl.ds(me * layers, layers)],
        regrouped.at[:, pl.ds(pl.multiple_of(me * rows, rows), rows), :],
        self_sem,
    )
    own.start()
    gram[...] = jnp.zeros_like(gram)
    own.wait()
    tiles = gram.shape[0] // TILE

    def step(c, carry):
        @pl.when(c + WINDOW < chunks)
        def _():
            send(c + WINDOW)

        for p in order:
            outgoing(c, p).wait_recv()
        layer, column = place(c)
        load = pltpu.make_async_copy(regrouped.at[layer, :, pl.ds(column, width)], block, load_sem)
        load.start()
        load.wait()

        @pl.loop(0, tiles)
        def _(i):
            first = pl.ds(pl.multiple_of(i * TILE, TILE), TILE)

            @pl.loop(i, tiles)
            def _(j):
                second = pl.ds(pl.multiple_of(j * TILE, TILE), TILE)
                gram[first, second] += dot(block[first, :], block[second, :], ((1,), (1,)))

        return carry

    lax.fori_loop(0, chunks, step, 0)

    def finish(c, carry):
        for p in order:
            outgoing(c, p).wait_send()
        return carry

    lax.fori_loop(0, chunks, finish, 0)

    @pl.loop(0, tiles)
    def _(i):
        first = pl.ds(pl.multiple_of(i * TILE, TILE), TILE)
        gram[first, first] = gram[first, first] * scale

        @pl.loop(i + 1, tiles)
        def _(j):
            second = pl.ds(pl.multiple_of(j * TILE, TILE), TILE)
            part = gram[first, second] * scale
            gram[first, second] = part
            gram[second, first] = part.T


def exchange_gram(demand, n, scale):
    total_layers, rows, columns = demand.shape
    layers = total_layers // n
    width = chunk_columns(layers, columns)
    chunks = layers * columns // width
    size = n * rows
    return pl.pallas_call(
        functools.partial(exchange_gram_kernel, n, layers, width, scale),
        out_shape=(
            jax.ShapeDtypeStruct((layers, size, columns), jnp.float32),
            jax.ShapeDtypeStruct((size, size), jnp.float32),
        ),
        in_specs=[pl.BlockSpec(memory_space=pl.ANY)],
        out_specs=(pl.BlockSpec(memory_space=pl.ANY), pl.BlockSpec(memory_space=pltpu.VMEM)),
        scratch_shapes=[
            pltpu.VMEM((size, width), jnp.float32),
            pltpu.SemaphoreType.DMA((chunks, n - 1)),
            pltpu.SemaphoreType.DMA((chunks, n - 1)),
            pltpu.SemaphoreType.DMA,
            pltpu.SemaphoreType.DMA,
        ],
        compiler_params=pltpu.CompilerParams(
            collective_id=0, has_side_effects=True, vmem_limit_bytes=40 * 2**20
        ),
        name="exchange_gram",
    )(demand)


def iterate_kernel(gram, initial, basis, image, work, inverse):
    size, rank = initial.shape
    lanes = 128
    basis[...] = initial[...]
    tiles = size // TILE

    def iteration(step, carry):
        work[:, :rank] = jnp.zeros((rank, rank), jnp.float32)

        @pl.loop(0, tiles)
        def _(i):
            rows = pl.ds(pl.multiple_of(i * TILE, TILE), TILE)
            part = dot(gram[rows, :], basis[...], ((1,), (0,)))
            image[rows, :] = part
            work[:, :rank] += dot(part, part, ((0,), (0,)))

        row = lax.broadcasted_iota(jnp.int32, (rank, rank), 0)
        column = lax.broadcasted_iota(jnp.int32, (rank, rank), 1)
        work[:, rank:] = (row == column).astype(jnp.float32)
        inverse[...] = jnp.zeros_like(inverse)
        index = lax.broadcasted_iota(jnp.int32, (PANEL, 1), 0)
        for k in range(0, rank, PANEL):
            low = k // lanes * lanes
            end = (k + PANEL - 1) // lanes * lanes + lanes
            panel = work[k : k + PANEL, low : rank + end]
            pivots = jnp.ones((PANEL, 1), jnp.float32)
            for j in range(PANEL):
                at = k + j - low
                pivot_column = panel[:, at : at + 1]
                pivot = pivot_column[j : j + 1, :]
                ratio = jnp.where(index > j, pivot_column / pivot, 0.0)
                pivots = jnp.where(index == j, pivot, pivots)
                panel = panel - ratio * panel[j : j + 1, :]
            panel = panel * (1.0 / jnp.sqrt(pivots))
            inverse[k : k + PANEL, :end] = panel[:, rank - low :]
            if k + PANEL < rank:
                update = dot(panel[:, : rank - low], panel, ((0,), (0,)))
                work[k + PANEL :, low : rank + end] -= update[k + PANEL - low :, :]

        @pl.loop(0, tiles)
        def _(i):
            rows = pl.ds(pl.multiple_of(i * TILE, TILE), TILE)
            basis[rows, :] = dot(image[rows, :], inverse[...], ((1,), (1,)))

        return carry

    lax.fori_loop(0, ITERS, iteration, 0)


def iterate(gram, initial):
    size, rank = initial.shape
    return pl.pallas_call(
        iterate_kernel,
        out_shape=jax.ShapeDtypeStruct((size, rank), jnp.float32),
        in_specs=[pl.BlockSpec(memory_space=pltpu.VMEM)] * 2,
        out_specs=pl.BlockSpec(memory_space=pltpu.VMEM),
        scratch_shapes=[
            pltpu.VMEM((size, rank), jnp.float32),
            pltpu.VMEM((rank, 2 * rank), jnp.float32),
            pltpu.VMEM((rank, rank), jnp.float32),
        ],
        compiler_params=pltpu.CompilerParams(vmem_limit_bytes=40 * 2**20),
        name="iterate",
    )(gram, initial)


def project_kernel(
    n, width, regrouped, basis, core, block, made, send_sems, recv_sems, self_sems, load_sems
):
    me = lax.axis_index("gx")
    layers, size, columns = regrouped.shape
    rank = basis.shape[1]
    share = rank // n
    per_layer = columns // width
    chunks = layers * per_layer
    order = far_first(n)

    def place(c):
        return lax.div(c, per_layer), pl.multiple_of(lax.rem(c, per_layer) * width, width)

    def load(c):
        layer, column = place(c)
        slot = lax.rem(c, 2)
        return pltpu.make_async_copy(
            regrouped.at[layer, :, pl.ds(column, width)], block.at[slot], load_sems.at[slot]
        )

    def outgoing(c, p):
        layer, column = place(c)
        target = lax.rem(me + p, n)
        return pltpu.make_async_remote_copy(
            src_ref=made.at[c, pl.ds(pl.multiple_of(target * share, share), share), :],
            dst_ref=core.at[me * layers + layer, :, pl.ds(column, width)],
            send_sem=send_sems.at[c, p - 1],
            recv_sem=recv_sems.at[c, p - 1],
            device_id={"gx": target},
            device_id_type=MESH,
        )

    def own(c):
        layer, column = place(c)
        return pltpu.make_async_copy(
            made.at[c, pl.ds(pl.multiple_of(me * share, share), share), :],
            core.at[me * layers + layer, :, pl.ds(column, width)],
            self_sems.at[c],
        )

    load(jnp.int32(0)).start()
    enter(n, me)

    def step(c, carry):
        slot = lax.rem(c, 2)

        @pl.when(c + 1 < chunks)
        def _():
            load(c + 1).start()

        load(c).wait()
        tile = min(width, TILE)

        @pl.loop(0, width // tile)
        def _(i):
            some = pl.ds(pl.multiple_of(i * tile, tile), tile)
            made[c, :, some] = dot(basis[...], block[slot, :, some], ((0,), (0,)))

        for p in order:
            outgoing(c, p).start()
        own(c).start()
        return carry

    lax.fori_loop(0, chunks, step, 0)

    def finish(c, carry):
        own(c).wait()
        for p in order:
            outgoing(c, p).wait()
        return carry

    lax.fori_loop(0, chunks, finish, 0)


def project(regrouped, basis, n):
    layers, size, columns = regrouped.shape
    rank = basis.shape[1]
    width = chunk_columns(layers, columns)
    chunks = layers * columns // width
    return pl.pallas_call(
        functools.partial(project_kernel, n, width),
        out_shape=jax.ShapeDtypeStruct((layers * n, rank // n, columns), jnp.float32),
        in_specs=[pl.BlockSpec(memory_space=pl.ANY), pl.BlockSpec(memory_space=pltpu.VMEM)],
        out_specs=pl.BlockSpec(memory_space=pl.ANY),
        scratch_shapes=[
            pltpu.VMEM((2, size, width), jnp.float32),
            pltpu.VMEM((chunks, rank, width), jnp.float32),
            pltpu.SemaphoreType.DMA((chunks, n - 1)),
            pltpu.SemaphoreType.DMA((chunks, n - 1)),
            pltpu.SemaphoreType.DMA((chunks,)),
            pltpu.SemaphoreType.DMA((2,)),
        ],
        compiler_params=pltpu.CompilerParams(
            collective_id=1, has_side_effects=True, vmem_limit_bytes=40 * 2**20
        ),
        name="project",
    )(regrouped, basis)


def on_device(n, groups, demand, initial):
    scale = 1.0 / (demand.shape[0] * demand.shape[2] * groups)
    regrouped, local_gram = exchange_gram(demand, n, scale)
    gram = lax.psum(local_gram, ("gx", "gy"))
    basis = iterate(gram, initial)
    core = project(regrouped, basis, n)
    return (basis, jnp.transpose(core, (1, 0, 2)))


def solution(mesh):
    in_specs = (P(None, "gx", "gy"), P())
    out_specs = (P(), P("gx", None, "gy"))
    return jax.shard_map(
        functools.partial(on_device, mesh.shape["gx"], mesh.shape["gy"]),
        mesh=mesh,
        in_specs=in_specs,
        out_specs=out_specs,
        check_vma=False,
    )
```

time: 1490 us -> 1200 us (0.81)
  Pallas kernels: 0 us -> 1030 us
  blocking collectives: 727 us -> 0 us
  matrix products: 178 us -> 0 us
  waiting for transfers between devices: 319 us -> 141 us
  other arithmetic: 164 us -> 0 us
  local copies, waits for them, and re-layouts: 54.2 us -> 13.7 us
  between operations: 31.3 us -> 14.1 us
    pallas_call x0 -> x3, Pallas kernels: none -> 1030 us  [the longest x1 739 us: exchange_gram(): pl.pallas_call(functools.partial(exchange_gram_kernel, n, layers, width,...]
    all_to_all x1 -> x0, blocking collectives: 727 us -> none  [on_device(): lax.all_to_all(demand, 'gx', split_axis=0, concat_axis=1, tiled=True)]
    all_to_all x1 -> x0, waiting for transfers between devices: 177 us -> none  [on_device(): lax.all_to_all(core_part, 'gx', split_axis=0, concat_axis=1, tiled=True)]
    dot_general x8 -> x0, matrix products: 170 us -> none  [the longest x1 115 us: on_device(): jnp.einsum('lxc,lzc->xz', regrouped, regrouped, precision=lax.Precision.H...]
    another operation x28 -> x0, other arithmetic: 164 us -> none  [the longest x20 103 us: orthonormal(): lower_factor = jnp.linalg.cholesky(weights)]
    all_to_all x3 -> x0, local copies, waits for them, and re-layouts: 29.3 us -> none  [the longest x2 18.3 us: on_device(): lax.all_to_all(core_part, 'gx', split_axis=0, concat_axis=1, tiled=True)]
  transfers between devices with their start and end apart: 2 -> 1, of which waited for: 2 -> 1; matrix products, arithmetic and copies ran while one was open for 0% -> 0% of each run, Pallas kernels for 0% -> 0%
where the time goes in v1:
time: 1200 us
  Pallas kernels  1030 us (86%)
  waiting for transfers between devices  141 us (12%)
  between operations  14.1 us (1%)
  local copies, waits for them, and re-layouts  13.7 us (1%)
    pallas_call x1, Pallas kernels, exchange_gram(): pl.pallas_call(functools.partial(exchange_gram_kernel, n, layers, width,...  739 us
    pallas_call x1, Pallas kernels, project(): pl.pallas_call(functools.partial(project_kernel, n, width), out_shape=jax...  189 us
    psum x1, waiting for transfers between devices, on_device(): gram = lax.psum(local_gram, ('gx', 'gy'))  141 us
    pallas_call x1, Pallas kernels, iterate(): pl.pallas_call(iterate_kernel, out_shape=jax.ShapeDtypeStruct((size, rank...  104 us
  transfers between devices with their start and end apart: 1, of which 1 were waited for; matrix products, arithmetic and copies ran while one was open for 0% of the time, Pallas kernels for 0%

profile of v1, /device:TPU:16, one launch (start us, length us, event | category | flops | bytes accessed | tf_op | source)
XLA Modules:
  0.0 1200.2 jit_solution(3749032820051551342)
XLA Ops:
  7.2 0.0 copy-start.3
  7.2 0.0 all-reduce.2.cloned.1.call-start
  7.2 739.2 %exchange_gram.1 = (f32[2,1024,4096]{2,1,0:T(8,128)}, f32[1024,1024]{1,0:T(8,128)S(1)}) custom-call(f32[16,128,4096]{2,1,0:T(8,128)} %demand.1), custom_call_target="tpu_custom_call" | custom-call | tf_op jit(solution)/shard_map/exchange_gram/pallas_call | solution.py:133
  746.4 0.0 copy-start.1
  746.4 2.0 copy-done.1
  748.4 0.0 all-reduce.2.cloned.1.call-update
  748.4 140.9 %all-reduce.2.cloned.1.call-done.gram = f32[1024,1024]{1,0:T(8,128)} async-done(((f32[1024,1024]{1,0:T(8,128)}), f32[1024,1024]{1,0:T(8,128)}) %all-reduce.2.cloned.1.call-update) | async-done | bytes 4194320 | tf_op jit(solution)/shard_map/psum | solution.py:324
  889.3 0.0 copy-done.3
  889.3 0.0 copy-start
  889.3 2.2 copy-done
  891.5 103.6 %iterate.1.basis = f32[1024,256]{1,0:T(8,128)} custom-call(f32[1024,1024]{1,0:T(8,128)S(1)} %copy-done, f32[1024,256]{1,0:T(8,128)S(1)} %copy-done.3), custom_call_target="tpu_custom_call" | custom-call | tf_op jit(solution)/shard_map/iterate/pallas_call | solution.py:206
  995.2 0.0 copy-start.2
  995.2 1.2 copy-done.2
  996.4 188.8 %project.1 = f32[16,32,4096]{2,1,0:T(8,128)S(1)} custom-call(f32[2,1024,4096]{2,1,0:T(8,128)} %get-tuple-element.5.regrouped, f32[1024,256]{1,0:T(8,128)S(1)} %copy-done.2), custom_call_target="tpu_custom_call" | custom-call | tf_op jit(solution)/shard_map/project/pallas_call | solution.py:301
  1185.1 8.3 copy.4
Async XLA Ops:
  7.2 882.2 %copy-start.3 = (f32[1024,256]{1,0:T(8,128)S(1)}, f32[1024,256]{1,0:T(8,128)}, u32[]{:S(2)}) copy-start(f32[1024,256]{1,0:T(8,128)} %initial.1) | copy-start | bytes 3145732
  7.2 882.2 %all-reduce.2.cloned.1.call-start = ((), (), s32[]{:S(2)}) async-start(), calls=%async_computation | async-start | bytes 8388608 | tf_op jit(solution)/shard_map/psum | solution.py:324
  746.4 2.0 copy-start.1
  889.3 2.2 copy-start
  995.2 1.2 copy-start.2
Sparse Core Ops, SparseCore 0:
  748.5 140.7 all-reduce.1

commit v2 on v1

--- a/solution.py
+++ b/solution.py
@@ -10,6 +10,7 @@
 ITERS = 3
 TILE = 256
 PANEL = 32
+GROUP = 8
 WINDOW = 3
 MESH = pl.DeviceIdType.MESH
 HIGHEST = lax.Precision.HIGHEST
@@ -36,6 +37,16 @@
             barrier, inc=1, device_id={"gx": lax.rem(me + p, n)}, device_id_type=MESH
         )
     pl.semaphore_wait(barrier, n - 1)
+
+
+def tile_row(tiles, i, j):
+    return (i * tiles - lax.div(i * (i - 1), 2) + j - i) * TILE
+
+
+def packed_rows(size, devices):
+    tiles = size // TILE
+    unit = 8 * devices
+    return -(-(tiles * (tiles + 1) // 2 * TILE) // unit) * unit
 
 
 def exchange_gram_kernel(
@@ -77,7 +88,7 @@
     own.start()
     gram[...] = jnp.zeros_like(gram)
     own.wait()
-    tiles = gram.shape[0] // TILE
+    tiles = n * rows // TILE
 
     def step(c, carry):
         @pl.when(c + WINDOW < chunks)
@@ -98,7 +109,8 @@
             @pl.loop(i, tiles)
             def _(j):
                 second = pl.ds(pl.multiple_of(j * TILE, TILE), TILE)
-                gram[first, second] += dot(block[first, :], block[second, :], ((1,), (1,)))
+                packed = pl.ds(pl.multiple_of(tile_row(tiles, i, j), TILE), TILE)
+                gram[packed, :] += dot(block[first, :], block[second, :], ((1,), (1,)))
 
         return carry
 
@@ -110,21 +122,10 @@
         return carry
 
     lax.fori_loop(0, chunks, finish, 0)
-
-    @pl.loop(0, tiles)
-    def _(i):
-        first = pl.ds(pl.multiple_of(i * TILE, TILE), TILE)
-        gram[first, first] = gram[first, first] * scale
-
-        @pl.loop(i + 1, tiles)
-        def _(j):
-            second = pl.ds(pl.multiple_of(j * TILE, TILE), TILE)
-            part = gram[first, second] * scale
-            gram[first, second] = part
-            gram[second, first] = part.T
-
-
-def exchange_gram(demand, n, scale):
+    gram[...] = gram[...] * scale
+
+
+def exchange_gram(demand, n, groups, scale):
     total_layers, rows, columns = demand.shape
     layers = total_layers // n
     width = chunk_columns(layers, columns)
@@ -134,7 +135,7 @@
         functools.partial(exchange_gram_kernel, n, layers, width, scale),
         out_shape=(
             jax.ShapeDtypeStruct((layers, size, columns), jnp.float32),
-            jax.ShapeDtypeStruct((size, size), jnp.float32),
+            jax.ShapeDtypeStruct((packed_rows(size, n * groups), TILE), jnp.float32),
         ),
         in_specs=[pl.BlockSpec(memory_space=pl.ANY)],
         out_specs=(pl.BlockSpec(memory_space=pl.ANY), pl.BlockSpec(memory_space=pltpu.VMEM)),
@@ -152,11 +153,155 @@
     )(demand)
 
 
-def iterate_kernel(gram, initial, basis, image, work, inverse):
+def sum_gram_kernel(
+    n, groups, local, out, total, half_in, half, quarter_in, quarter, piece_in, send_sems, recv_sems
+):
+    me = lax.axis_index("gx")
+    group = lax.axis_index("gy")
+    z, core = lax.div(me, 2), lax.rem(me, 2)
+    depth = n // 2
+    mate = me + 1 - 2 * core
+    half_rows = local.shape[0] // 2
+    quarter_rows = half_rows // groups
+    piece_rows = quarter_rows // depth
+
+    def copy(src, dst, slot, device):
+        return pltpu.make_async_remote_copy(
+            src_ref=src,
+            dst_ref=dst,
+            send_sem=send_sems.at[slot],
+            recv_sem=recv_sems.at[slot],
+            device_id=device,
+            device_id_type=MESH,
+        )
+
+    def rows(start, count):
+        return pl.ds(pl.multiple_of(start, 8), count)
+
+    def along_gy(q):
+        return lax.rem(group + q, groups)
+
+    def along_z(q):
+        return lax.rem(z + q, depth)
+
+    def gy_device(q):
+        return {"gx": me, "gy": along_gy(q)}
+
+    def z_device(q):
+        return {"gx": along_z(q) * 2 + core, "gy": group}
+
+    mate_device = {"gx": mate, "gy": group}
+    barrier = pltpu.get_barrier_semaphore()
+    near = [mate_device]
+    near += [gy_device(q) for q in range(1, groups)]
+    near += [z_device(q) for q in range(1, depth)]
+    for device in near:
+        pl.semaphore_signal(barrier, inc=1, device_id=device, device_id_type=MESH)
+    pl.semaphore_wait(barrier, len(near))
+
+    first = copy(local.at[rows((1 - core) * half_rows, half_rows)], half_in, 0, mate_device)
+    first.start()
+    first.wait()
+    half[...] = local[rows(core * half_rows, half_rows), :] + half_in[...]
+    slot = 1
+    seconds = []
+    for q in range(1, groups):
+        part = half.at[rows(along_gy(q) * quarter_rows, quarter_rows)]
+        seconds.append(copy(part, quarter_in.at[q - 1], slot, gy_device(q)))
+        seconds[-1].start()
+        slot += 1
+    value = half[rows(group * quarter_rows, quarter_rows), :]
+    for q in range(1, groups):
+        seconds[q - 1].wait()
+        value = value + quarter_in[q - 1]
+    quarter[...] = value
+    thirds = []
+    for q in range(1, depth):
+        part = quarter.at[rows(along_z(q) * piece_rows, piece_rows)]
+        thirds.append(copy(part, piece_in.at[q - 1], slot, z_device(q)))
+        thirds[-1].start()
+        slot += 1
+    value = quarter[rows(z * piece_rows, piece_rows), :]
+    for q in range(1, depth):
+        thirds[q - 1].wait()
+        value = value + piece_in[q - 1]
+
+    base = core * half_rows
+    mine = base + group * quarter_rows
+    total[rows(mine + z * piece_rows, piece_rows), :] = value
+    piece = total.at[rows(mine + z * piece_rows, piece_rows)]
+    fourths = []
+    for q in range(1, depth):
+        fourths.append(copy(piece, piece, slot, z_device(q)))
+        fourths[-1].start()
+        slot += 1
+    for done in fourths:
+        done.wait()
+    own_quarter = total.at[rows(mine, quarter_rows)]
+    fifths = []
+    for q in range(1, groups):
+        fifths.append(copy(own_quarter, own_quarter, slot, gy_device(q)))
+        fifths[-1].start()
+        slot += 1
+    lasts = [copy(own_quarter, own_quarter, slot, mate_device)]
+    lasts[0].start()
+    slot += 1
+    for q in range(1, groups):
+        fifths[q - 1].wait()
+        source = lax.rem(group + groups - q, groups)
+        part = total.at[rows(base + source * quarter_rows, quarter_rows)]
+        lasts.append(copy(part, part, slot, mate_device))
+        lasts[-1].start()
+        slot += 1
+    for done in lasts:
+        done.wait()
+    out[...] = total[...]
+
+
+def sum_gram(local, n, groups):
+    rows, lanes = local.shape
+    half, quarter, piece = rows // 2, rows // 2 // groups, rows // n // groups
+    copies = 1 + 2 * (groups - 1) + 2 * (n // 2 - 1) + groups
+    return pl.pallas_call(
+        functools.partial(sum_gram_kernel, n, groups),
+        out_shape=jax.ShapeDtypeStruct((rows, lanes), jnp.float32),
+        in_specs=[pl.BlockSpec(memory_space=pltpu.VMEM)],
+        out_specs=pl.BlockSpec(memory_space=pltpu.VMEM),
+        scratch_shapes=[
+            pltpu.VMEM((rows, lanes), jnp.float32),
+            pltpu.VMEM((half, lanes), jnp.float32),
+            pltpu.VMEM((half, lanes), jnp.float32),
+            pltpu.VMEM((groups - 1, quarter, lanes), jnp.float32),
+            pltpu.VMEM((quarter, lanes), jnp.float32),
+            pltpu.VMEM((n // 2 - 1, piece, lanes), jnp.float32),
+            pltpu.SemaphoreType.DMA((copies,)),
+            pltpu.SemaphoreType.DMA((copies,)),
+        ],
+        compiler_params=pltpu.CompilerParams(
+            collective_id=2, has_side_effects=True, vmem_limit_bytes=40 * 2**20
+        ),
+        name="sum_gram",
+    )(local)
+
+
+def iterate_kernel(packed, initial, basis, gram, image, work, inverse):
     size, rank = initial.shape
     lanes = 128
     basis[...] = initial[...]
     tiles = size // TILE
+
+    @pl.loop(0, tiles)
+    def _(i):
+        first = pl.ds(pl.multiple_of(i * TILE, TILE), TILE)
+        diagonal = pl.ds(pl.multiple_of(tile_row(tiles, i, i), TILE), TILE)
+        gram[first, first] = packed[diagonal, :]
+
+        @pl.loop(i + 1, tiles)
+        def _(j):
+            second = pl.ds(pl.multiple_of(j * TILE, TILE), TILE)
+            part = packed[pl.ds(pl.multiple_of(tile_row(tiles, i, j), TILE), TILE), :]
+            gram[first, second] = part
+            gram[second, first] = part.T
 
     def iteration(step, carry):
         work[:, :rank] = jnp.zeros((rank, rank), jnp.float32)
@@ -172,20 +317,31 @@
         column = lax.broadcasted_iota(jnp.int32, (rank, rank), 1)
         work[:, rank:] = (row == column).astype(jnp.float32)
         inverse[...] = jnp.zeros_like(inverse)
-        index = lax.broadcasted_iota(jnp.int32, (PANEL, 1), 0)
+        index = lax.broadcasted_iota(jnp.int32, (PANEL, lanes), 0)
         for k in range(0, rank, PANEL):
             low = k // lanes * lanes
             end = (k + PANEL - 1) // lanes * lanes + lanes
-            panel = work[k : k + PANEL, low : rank + end]
-            pivots = jnp.ones((PANEL, 1), jnp.float32)
-            for j in range(PANEL):
-                at = k + j - low
-                pivot_column = panel[:, at : at + 1]
-                pivot = pivot_column[j : j + 1, :]
-                ratio = jnp.where(index > j, pivot_column / pivot, 0.0)
-                pivots = jnp.where(index == j, pivot, pivots)
-                panel = panel - ratio * panel[j : j + 1, :]
-            panel = panel * (1.0 / jnp.sqrt(pivots))
+            strips = [
+                work[k : k + PANEL, at : at + lanes] for at in range(low, rank + end, lanes)
+            ]
+            pivots = jnp.ones((PANEL, lanes), jnp.float32)
+            for start in range(0, PANEL, GROUP):
+                ahead = []
+                for j in range(start, start + GROUP):
+                    strip, at = divmod(k + j - low, lanes)
+                    ahead.append(
+                        jnp.broadcast_to(strips[strip][:, at : at + 1], (PANEL, lanes))
+                    )
+                for j in range(start, start + GROUP):
+                    current = ahead[j - start]
+                    pivot = current[j : j + 1, :]
+                    ratio = jnp.where(index > j, current * (1.0 / pivot), 0.0)
+                    pivots = jnp.where(index == j, pivot, pivots)
+                    for t in range(j - start + 1, GROUP):
+                        ahead[t] = ahead[t] - ratio * ahead[t][j : j + 1, :]
+                    strips = [strip - ratio * strip[j : j + 1, :] for strip in strips]
+            root = 1.0 / jnp.sqrt(pivots)
+            panel = jnp.concatenate([strip * root for strip in strips], axis=1)
             inverse[k : k + PANEL, :end] = panel[:, rank - low :]
             if k + PANEL < rank:
                 update = dot(panel[:, : rank - low], panel, ((0,), (0,)))
@@ -201,7 +357,7 @@
     lax.fori_loop(0, ITERS, iteration, 0)
 
 
-def iterate(gram, initial):
+def iterate(packed, initial):
     size, rank = initial.shape
     return pl.pallas_call(
         iterate_kernel,
@@ -209,13 +365,14 @@
         in_specs=[pl.BlockSpec(memory_space=pltpu.VMEM)] * 2,
         out_specs=pl.BlockSpec(memory_space=pltpu.VMEM),
         scratch_shapes=[
+            pltpu.VMEM((size, size), jnp.float32),
             pltpu.VMEM((size, rank), jnp.float32),
             pltpu.VMEM((rank, 2 * rank), jnp.float32),
             pltpu.VMEM((rank, rank), jnp.float32),
         ],
         compiler_params=pltpu.CompilerParams(vmem_limit_bytes=40 * 2**20),
         name="iterate",
-    )(gram, initial)
+    )(packed, initial)
 
 
 def project_kernel(
@@ -320,9 +477,8 @@
 
 def on_device(n, groups, demand, initial):
     scale = 1.0 / (demand.shape[0] * demand.shape[2] * groups)
-    regrouped, local_gram = exchange_gram(demand, n, scale)
-    gram = lax.psum(local_gram, ("gx", "gy"))
-    basis = iterate(gram, initial)
+    regrouped, local_gram = exchange_gram(demand, n, groups, scale)
+    basis = iterate(sum_gram(local_gram, n, groups), initial)
     core = project(regrouped, basis, n)
     return (basis, jnp.transpose(core, (1, 0, 2)))
 

time: 1200 us -> 1050 us (0.88)
  waiting for transfers between devices: 141 us -> 0 us
  between operations: 14.1 us -> 0.67 us
    psum x1 -> x0, waiting for transfers between devices: 141 us -> none  [on_device(): gram = lax.psum(local_gram, ('gx', 'gy'))]
    pallas_call x0 -> x1, Pallas kernels: none -> 55.2 us  [sum_gram(): pl.pallas_call(functools.partial(sum_gram_kernel, n, groups), out_shape=j...]
    pallas_call x1, Pallas kernels: 104 us -> 57.5 us  [iterate(): pl.pallas_call(iterate_kernel, out_shape=jax.ShapeDtypeStruct((size, rank...]
  transfers between devices with their start and end apart: 1 -> 0, of which waited for: 1 -> 0; matrix products, arithmetic and copies ran while one was open for 0% -> 0% of each run, Pallas kernels for 0% -> 0%
where the time goes in v2:
time: 1050 us
  Pallas kernels  1040 us (99%)
    pallas_call x1, Pallas kernels, exchange_gram(): pl.pallas_call(functools.partial(exchange_gram_kernel, n, layers, width,...  738 us
    pallas_call x1, Pallas kernels, project(): pl.pallas_call(functools.partial(project_kernel, n, width), out_shape=jax...  191 us
    pallas_call x1, Pallas kernels, iterate(): pl.pallas_call(iterate_kernel, out_shape=jax.ShapeDtypeStruct((size, rank...  57.5 us
    pallas_call x1, Pallas kernels, sum_gram(): pl.pallas_call(functools.partial(sum_gram_kernel, n, groups), out_shape=j...  55.2 us

profile of v2, /device:TPU:16, one launch (start us, length us, event | category | flops | bytes accessed | tf_op | source)
XLA Modules:
  0.0 1052.5 jit_solution(14926796494351246725)
XLA Ops:
  0.6 0.0 copy-start.1
  0.6 738.3 %exchange_gram.1 = (f32[2,1024,4096]{2,1,0:T(8,128)}, f32[2560,256]{1,0:T(8,128)S(1)}) custom-call(f32[16,128,4096]{2,1,0:T(8,128)} %demand.1), custom_call_target="tpu_custom_call" | custom-call | tf_op jit(solution)/shard_map/exchange_gram/pallas_call | solution.py:134
  739.0 55.2 %sum_gram.1.packed = f32[2560,256]{1,0:T(8,128)S(1)} custom-call(f32[2560,256]{1,0:T(8,128)S(1)} %get-tuple-element.4.local), custom_call_target="tpu_custom_call" | custom-call | tf_op jit(solution)/shard_map/sum_gram/pallas_call | solution.py:265
  794.2 0.0 copy-done.1
  794.2 57.5 %iterate.1.basis = f32[1024,256]{1,0:T(8,128)} custom-call(f32[2560,256]{1,0:T(8,128)S(1)} %sum_gram.1.packed, f32[1024,256]{1,0:T(8,128)S(1)} %copy-done.1), custom_call_target="tpu_custom_call" | custom-call | tf_op jit(solution)/shard_map/iterate/pallas_call | solution.py:362
  851.7 0.0 copy-start
  851.7 1.2 copy-done
  852.9 191.3 %project.1 = f32[16,32,4096]{2,1,0:T(8,128)S(1)} custom-call(f32[2,1024,4096]{2,1,0:T(8,128)} %get-tuple-element.5.regrouped, f32[1024,256]{1,0:T(8,128)S(1)} %copy-done), custom_call_target="tpu_custom_call" | custom-call | tf_op jit(solution)/shard_map/project/pallas_call | solution.py:458
  1044.3 8.3 copy.4
Async XLA Ops:
  0.6 793.5 %copy-start.1 = (f32[1024,256]{1,0:T(8,128)S(1)}, f32[1024,256]{1,0:T(8,128)}, u32[]{:S(2)}) copy-start(f32[1024,256]{1,0:T(8,128)} %initial.1) | copy-start | bytes 3145732
  851.7 1.2 copy-start

commit v3 on v2

--- a/solution.py
+++ b/solution.py
@@ -11,7 +11,7 @@
 TILE = 256
 PANEL = 32
 GROUP = 8
-WINDOW = 3
+WINDOW = 6
 MESH = pl.DeviceIdType.MESH
 HIGHEST = lax.Precision.HIGHEST
 
@@ -23,7 +23,7 @@
 
 
 def chunk_columns(layers, columns):
-    return min(columns, max(128, layers * columns // 8))
+    return min(columns, max(128, layers * columns // 16))
 
 
 def far_first(n):
@@ -45,7 +45,7 @@
 
 def packed_rows(size, devices):
     tiles = size // TILE
-    unit = 8 * devices
+    unit = 16 * devices
     return -(-(tiles * (tiles + 1) // 2 * TILE) // unit) * unit
 
 
@@ -154,7 +154,8 @@
 
 
 def sum_gram_kernel(
-    n, groups, local, out, total, half_in, half, quarter_in, quarter, piece_in, send_sems, recv_sems
+    n, groups, local, out, total, half_in, half, gy_wide, z_narrow, z_wide, gy_narrow,
+    middle_gy, middle_z, send_sems, recv_sems
 ):
     me = lax.axis_index("gx")
     group = lax.axis_index("gy")
@@ -162,11 +163,14 @@
     depth = n // 2
     mate = me + 1 - 2 * core
     half_rows = local.shape[0] // 2
-    quarter_rows = half_rows // groups
-    piece_rows = quarter_rows // depth
-
-    def copy(src, dst, slot, device):
-        return pltpu.make_async_remote_copy(
+    track_rows = half_rows // 2
+    piece_rows = track_rows // groups // depth
+    used = [0]
+
+    def copy(src, dst, device):
+        slot = used[0]
+        used[0] += 1
+        started = pltpu.make_async_remote_copy(
             src_ref=src,
             dst_ref=dst,
             send_sem=send_sems.at[slot],
@@ -174,6 +178,8 @@
             device_id=device,
             device_id_type=MESH,
         )
+        started.start()
+        return started
 
     def rows(start, count):
         return pl.ds(pl.multiple_of(start, 8), count)
@@ -199,69 +205,88 @@
         pl.semaphore_signal(barrier, inc=1, device_id=device, device_id_type=MESH)
     pl.semaphore_wait(barrier, len(near))
 
-    first = copy(local.at[rows((1 - core) * half_rows, half_rows)], half_in, 0, mate_device)
-    first.start()
+    gy_axis = (groups, group, along_gy, gy_device)
+    z_axis = (depth, z, along_z, z_device)
+
+    def scatter(source, offset, count, landing, axis):
+        size, _, along, device = axis
+        part = count // size
+        return [
+            copy(source.at[rows(offset + along(q) * part, part)], landing.at[q - 1], device(q))
+            for q in range(1, size)
+        ]
+
+    def collect(copies, source, offset, count, landing, axis):
+        size, here, _, _ = axis
+        part = count // size
+        value = source[rows(offset + here * part, part), :]
+        for q in range(1, size):
+            copies[q - 1].wait()
+            value = value + landing[q - 1]
+        return value
+
+    def spread(start, count, axis):
+        part = total.at[rows(start, count)]
+        return [copy(part, part, axis[3](q)) for q in range(1, axis[0])]
+
+    def wait(copies):
+        for done in copies:
+            done.wait()
+
+    first = copy(local.at[rows((1 - core) * half_rows, half_rows)], half_in, mate_device)
     first.wait()
     half[...] = local[rows(core * half_rows, half_rows), :] + half_in[...]
-    slot = 1
-    seconds = []
-    for q in range(1, groups):
-        part = half.at[rows(along_gy(q) * quarter_rows, quarter_rows)]
-        seconds.append(copy(part, quarter_in.at[q - 1], slot, gy_device(q)))
-        seconds[-1].start()
-        slot += 1
-    value = half[rows(group * quarter_rows, quarter_rows), :]
-    for q in range(1, groups):
-        seconds[q - 1].wait()
-        value = value + quarter_in[q - 1]
-    quarter[...] = value
-    thirds = []
-    for q in range(1, depth):
-        part = quarter.at[rows(along_z(q) * piece_rows, piece_rows)]
-        thirds.append(copy(part, piece_in.at[q - 1], slot, z_device(q)))
-        thirds[-1].start()
-        slot += 1
-    value = quarter[rows(z * piece_rows, piece_rows), :]
-    for q in range(1, depth):
-        thirds[q - 1].wait()
-        value = value + piece_in[q - 1]
-
-    base = core * half_rows
-    mine = base + group * quarter_rows
-    total[rows(mine + z * piece_rows, piece_rows), :] = value
-    piece = total.at[rows(mine + z * piece_rows, piece_rows)]
-    fourths = []
-    for q in range(1, depth):
-        fourths.append(copy(piece, piece, slot, z_device(q)))
-        fourths[-1].start()
-        slot += 1
-    for done in fourths:
-        done.wait()
-    own_quarter = total.at[rows(mine, quarter_rows)]
-    fifths = []
-    for q in range(1, groups):
-        fifths.append(copy(own_quarter, own_quarter, slot, gy_device(q)))
-        fifths[-1].start()
-        slot += 1
-    lasts = [copy(own_quarter, own_quarter, slot, mate_device)]
-    lasts[0].start()
-    slot += 1
-    for q in range(1, groups):
-        fifths[q - 1].wait()
-        source = lax.rem(group + groups - q, groups)
-        part = total.at[rows(base + source * quarter_rows, quarter_rows)]
-        lasts.append(copy(part, part, slot, mate_device))
-        lasts[-1].start()
-        slot += 1
-    for done in lasts:
-        done.wait()
+    wide_a = scatter(half, 0, track_rows, gy_wide, gy_axis)
+    wide_b = scatter(half, track_rows, track_rows, z_wide, z_axis)
+    gy_rows, z_rows = track_rows // groups, track_rows // depth
+    middle_gy[...] = collect(wide_a, half, 0, track_rows, gy_wide, gy_axis)
+    narrow_a = scatter(middle_gy, 0, gy_rows, z_narrow, z_axis)
+    middle_z[...] = collect(wide_b, half, track_rows, track_rows, z_wide, z_axis)
+    narrow_b = scatter(middle_z, 0, z_rows, gy_narrow, gy_axis)
+
+    base_a = core * half_rows
+    base_b = base_a + track_rows
+    part_a = base_a + group * gy_rows
+    part_b = base_b + z * z_rows
+    piece_a = part_a + z * piece_rows
+    piece_b = part_b + group * piece_rows
+    total[rows(piece_a, piece_rows), :] = collect(
+        narrow_a, middle_gy, 0, gy_rows, z_narrow, z_axis
+    )
+    back_a = spread(piece_a, piece_rows, z_axis)
+    total[rows(piece_b, piece_rows), :] = collect(
+        narrow_b, middle_z, 0, z_rows, gy_narrow, gy_axis
+    )
+    back_b = spread(piece_b, piece_rows, gy_axis)
+    wait(back_a)
+    wide_a = spread(part_a, gy_rows, gy_axis)
+    mine_a = total.at[rows(part_a, gy_rows)]
+    lasts = [copy(mine_a, mine_a, mate_device)]
+    wait(back_b)
+    wide_b = spread(part_b, z_rows, z_axis)
+    mine_b = total.at[rows(part_b, z_rows)]
+    lasts.append(copy(mine_b, mine_b, mate_device))
+
+    def hand_on(copies, base, count, axis):
+        size, here, _, _ = axis
+        for q in range(1, size):
+            copies[q - 1].wait()
+            source = lax.rem(here + size - q, size)
+            part = total.at[rows(base + source * count, count)]
+            lasts.append(copy(part, part, mate_device))
+
+    hand_on(wide_a, base_a, gy_rows, gy_axis)
+    hand_on(wide_b, base_b, z_rows, z_axis)
+    wait(lasts)
     out[...] = total[...]
 
 
 def sum_gram(local, n, groups):
     rows, lanes = local.shape
-    half, quarter, piece = rows // 2, rows // 2 // groups, rows // n // groups
-    copies = 1 + 2 * (groups - 1) + 2 * (n // 2 - 1) + groups
+    depth = n // 2
+    half, track = rows // 2, rows // 4
+    piece = track // groups // depth
+    copies = 1 + 4 * (groups - 1) + 4 * (depth - 1) + groups + depth
     return pl.pallas_call(
         functools.partial(sum_gram_kernel, n, groups),
         out_shape=jax.ShapeDtypeStruct((rows, lanes), jnp.float32),
@@ -271,9 +296,12 @@
             pltpu.VMEM((rows, lanes), jnp.float32),
             pltpu.VMEM((half, lanes), jnp.float32),
             pltpu.VMEM((half, lanes), jnp.float32),
-            pltpu.VMEM((groups - 1, quarter, lanes), jnp.float32),
-            pltpu.VMEM((quarter, lanes), jnp.float32),
-            pltpu.VMEM((n // 2 - 1, piece, lanes), jnp.float32),
+            pltpu.VMEM((groups - 1, track // groups, lanes), jnp.float32),
+            pltpu.VMEM((depth - 1, piece, lanes), jnp.float32),
+            pltpu.VMEM((depth - 1, track // depth, lanes), jnp.float32),
+            pltpu.VMEM((groups - 1, piece, lanes), jnp.float32),
+            pltpu.VMEM((track // groups, lanes), jnp.float32),
+            pltpu.VMEM((track // depth, lanes), jnp.float32),
             pltpu.SemaphoreType.DMA((copies,)),
             pltpu.SemaphoreType.DMA((copies,)),
         ],

time: 1050 us -> 1040 us (level)
  no operation moved by 1% of the time
where the time goes in v3:
time: 1040 us
  Pallas kernels  1030 us (99%)
    pallas_call x1, Pallas kernels, exchange_gram(): pl.pallas_call(functools.partial(exchange_gram_kernel, n, layers, width,...  734 us
    pallas_call x1, Pallas kernels, project(): pl.pallas_call(functools.partial(project_kernel, n, width), out_shape=jax...  190 us
    pallas_call x1, Pallas kernels, iterate(): pl.pallas_call(iterate_kernel, out_shape=jax.ShapeDtypeStruct((size, rank...  57.5 us
    pallas_call x1, Pallas kernels, sum_gram(): pl.pallas_call(functools.partial(sum_gram_kernel, n, groups), out_shape=j...  45.3 us

profile of v3, /device:TPU:16, one launch (start us, length us, event | category | flops | bytes accessed | tf_op | source)
XLA Modules:
  0.0 1037.4 jit_solution(1231173790670438179)
XLA Ops:
  0.6 0.0 copy-start.1
  0.6 734.4 %exchange_gram.1 = (f32[2,1024,4096]{2,1,0:T(8,128)}, f32[2560,256]{1,0:T(8,128)S(1)}) custom-call(f32[16,128,4096]{2,1,0:T(8,128)} %demand.1), custom_call_target="tpu_custom_call" | custom-call | tf_op jit(solution)/shard_map/exchange_gram/pallas_call | solution.py:134
  735.1 45.3 %sum_gram.1.packed = f32[2560,256]{1,0:T(8,128)S(1)} custom-call(f32[2560,256]{1,0:T(8,128)S(1)} %get-tuple-element.4.local), custom_call_target="tpu_custom_call" | custom-call | tf_op jit(solution)/shard_map/sum_gram/pallas_call | solution.py:290
  780.4 0.0 copy-done.1
  780.4 57.5 %iterate.1.basis = f32[1024,256]{1,0:T(8,128)} custom-call(f32[2560,256]{1,0:T(8,128)S(1)} %sum_gram.1.packed, f32[1024,256]{1,0:T(8,128)S(1)} %copy-done.1), custom_call_target="tpu_custom_call" | custom-call | tf_op jit(solution)/shard_map/iterate/pallas_call | solution.py:390
  837.9 0.0 copy-start
  837.9 1.2 copy-done
  839.2 189.9 %project.1 = f32[16,32,4096]{2,1,0:T(8,128)S(1)} custom-call(f32[2,1024,4096]{2,1,0:T(8,128)} %get-tuple-element.5.regrouped, f32[1024,256]{1,0:T(8,128)S(1)} %copy-done), custom_call_target="tpu_custom_call" | custom-call | tf_op jit(solution)/shard_map/project/pallas_call | solution.py:486
  1029.1 8.3 copy.4
Async XLA Ops:
  0.6 779.8 %copy-start.1 = (f32[1024,256]{1,0:T(8,128)S(1)}, f32[1024,256]{1,0:T(8,128)}, u32[]{:S(2)}) copy-start(f32[1024,256]{1,0:T(8,128)} %initial.1) | copy-start | bytes 3145732
  837.9 1.2 copy-start
